TPU v7x, 512 devices: a whole 4x4x16 slice. The times are simulated.
512 devices in a mesh: span: 8 (over z_lo, core), seq: 64 (over y, x, z_hi).
Axes of the slice: x: 4, y: 4, z: 16 (z_hi: 4, z_lo: 4; z = z_hi * 4 + z_lo), core: 2. Of those that a mesh axis runs over, the one named last changes fastest.
Arguments:
- query_rows: bfloat16 [8, 512, 4096], P('span', 'seq'), may hold values from -6 to 6
- key_rows: bfloat16 [8, 512, 4096], P('span', 'seq'), may hold values from -6 to 6
- value_rows: bfloat16 [8, 512, 4096], P('span', 'seq'), may hold values from -6 to 6
- counts: int32 [8], replicated, may hold values from 128 to 512, as said below
- levels: int32 [8], replicated, may hold values from 0 to 63
- gate_table: float32 [64, 4096], replicated, may hold values from 0.1 to 1.9
Outputs:
- mixed_rows: bfloat16 [8, 512, 4096], P('span', 'seq')
Inputs may be any that keep to these rules, and one draw needn't show every extreme that they name: `counts`: some span has all 512 tokens live in every draw.
All inputs are finite; a program needn't handle non-finite values.
Results may differ from a plain program's by a relative error of at most 0.0075.
Values may be sent and summed in bfloat16 or wider, within the bound.
A program may use at most 64 MiB of HBM per device.

v0:
```python
import math

import jax
import jax.numpy as jnp
from jax import lax
from jax.sharding import PartitionSpec as P

HEADS = 32
HEAD_DIM = 128


masked_score = -1e30
epsilon = 1e-05


def pick_entry(table, wanted):
    return jnp.sum(jnp.where(jnp.arange(table.shape[0], dtype=jnp.int32) == wanted, table, 0))


def body(query_rows, key_rows, value_rows, counts, levels, gate_table):
    seq_size = lax.axis_size("seq")
    tok_rows = query_rows.shape[1]
    groups = min(HEADS, seq_size)
    copies = seq_size // groups
    per_dev = HEADS // groups
    channels = per_dev * HEAD_DIM
    part_rows = tok_rows // copies
    span_tok = tok_rows * seq_size
    query_count = seq_size * part_rows
    my_span = lax.axis_index("span")
    my_group = lax.axis_index("seq") // copies
    score_scale = 1.0 / math.sqrt(HEAD_DIM)

    def head_layout(row_block):
        lead_dim = row_block.shape[0]
        grouped = row_block.reshape(lead_dim, tok_rows, groups, channels).transpose(0, 2, 1, 3)
        return jnp.repeat(grouped, copies, axis=1)

    query_send = query_rows[0].reshape(copies, part_rows, groups, channels).transpose(2, 0, 1, 3)
    query_send = query_send.reshape(query_count, channels)
    query_heads = lax.all_to_all(query_send, "seq", split_axis=0, concat_axis=0, tiled=True)
    query_heads = query_heads.reshape(query_count, per_dev, HEAD_DIM)
    positions = jnp.arange(span_tok, dtype=jnp.int32)
    start_state = (
        jnp.full((per_dev, query_count), masked_score, jnp.float32),
        jnp.zeros((per_dev, query_count), jnp.float32),
        jnp.zeros((per_dev, query_count, HEAD_DIM), jnp.float32),
    )
    all_keys, all_values = (
        lax.all_gather(key_rows, "span", axis=0, tiled=True),
        lax.all_gather(value_rows, "span", axis=0, tiled=True),
    )
    key_heads, value_heads = (
        lax.all_to_all(head_layout(all_keys), "seq", split_axis=1, concat_axis=1, tiled=True),
        lax.all_to_all(head_layout(all_values), "seq", split_axis=1, concat_axis=1, tiled=True),
    )
    span_total = key_heads.shape[0]
    carry_state = start_state
    pieces = (
        key_heads.reshape(span_total, span_tok, channels),
        value_heads.reshape(span_total, span_tok, channels),
    )
    for offset in range(pieces[0].shape[0]):
        key_block = pieces[0][offset]
        value_block = pieces[1][offset]
        span_id = 0 + offset
        run_max, add_run_total, add_run_sum = carry_state
        allowed = (span_id <= my_span) & (positions < pick_entry(counts, span_id))
        key_block = key_block.reshape(span_tok, per_dev, HEAD_DIM)
        value_block = value_block.reshape(span_tok, per_dev, HEAD_DIM)
        scores = (
            jnp.einsum("qhd,khd->hqk", query_heads, key_block, preferred_element_type=jnp.float32)
            * score_scale
        )
        scores = jnp.where(allowed[None, None, :], scores, masked_score)
        new_max = jnp.maximum(run_max, jnp.max(scores, axis=2))
        shrink = jnp.exp(run_max - new_max)
        weights = jnp.where(allowed[None, None, :], jnp.exp(scores - new_max[:, :, None]), 0.0)
        add_run_total = add_run_total * shrink + jnp.sum(weights, axis=2)
        added = jnp.einsum(
            "hqk,khd->hqd",
            weights.astype(jnp.bfloat16),
            value_block,
            preferred_element_type=jnp.float32,
        )
        add_run_sum = add_run_sum * shrink[:, :, None] + added
        carry_state = (new_max, add_run_total, add_run_sum)
    run_total = carry_state[1]
    run_sum = carry_state[2]
    attended = run_sum / run_total[:, :, None]
    normed = attended * lax.rsqrt(jnp.mean(attended * attended, axis=2, keepdims=True) + epsilon)
    my_level = pick_entry(levels, my_span)
    chooser = (jnp.arange(gate_table.shape[0], dtype=jnp.int32) == my_level).astype(jnp.float32)[
        None, :
    ]
    gate_row = jnp.dot(chooser, gate_table, precision=lax.Precision.HIGHEST)
    gate_heads = lax.dynamic_slice_in_dim(gate_row[0], my_group * channels, channels).reshape(
        per_dev, 1, HEAD_DIM
    )
    mixed_heads = (normed * gate_heads).astype(jnp.bfloat16)
    mixed_send = mixed_heads.transpose(1, 0, 2).reshape(query_count, channels)
    returned = lax.all_to_all(mixed_send, "seq", split_axis=0, concat_axis=0, tiled=True)
    mixed_rows = returned.reshape(groups, copies, part_rows, channels).transpose(1, 2, 0, 3)
    return mixed_rows.reshape(1, tok_rows, groups * channels)


def solution(mesh):
    placed = (P("span", "seq", None), P("span", "seq", None), P("span", "seq", None), P(), P(), P())
    return jax.shard_map(
        body, mesh=mesh, in_specs=placed, out_specs=P("span", "seq", None), check_vma=False
    )
```

profile of v0, /device:TPU:1, one launch (start us, length us, event | category | flops | bytes accessed | tf_op | source)
XLA Modules:
  0.0 223.8 jit_solution(17831453119307198601)
XLA Ops:
  0.0 0.0 copy-start
  0.0 0.9 copy.18
  0.9 0.1 copy.13
  1.0 0.7 copy.14
  1.7 21.9 %all-to-all-start = ((bf16[64,4,128]{2,1,0:T(4,128)(2,1)}), bf16[64,4,128]{2,1,0:T(4,128)(2,1)S(1)}, u32[]{:S(2)}, u32[]{:S(2)}) async-start(bf16[64,4,128]{2,1,0:T(4,128)(2,1)} %copy.14), calls=%async_computation | async-start | bytes 131072 | tf_op jit(solution)/shard_map/all_to_all | solution.py:41
  23.6 0.0 copy-done.9
  23.6 16.7 %all_gather.6 = bf16[8,8,4096]{2,1,0:T(8,128)(2,1)S(1)} all-gather(bf16[1,8,4096]{2,1,0:T(8,128)(2,1)S(1)} %copy-done.9), channel_id=1, replica_groups=mesh['span'=8,'seq'=64] {'span'}, dimensions={0}, use_global_device_ids=true | all-gather | bytes 589824 | tf_op jit(solution)/shard_map/all_gather | solution.py:50
  40.3 0.1 copy.15
  40.5 0.0 all-to-all-done
  40.5 1.3 broadcast_in_dim.148
  41.8 16.4 %all-to-all-start.1 = ((bf16[8,64,8,128]{3,2,0,1:T(8,128)(2,1)}), bf16[8,64,8,128]{3,2,0,1:T(8,128)(2,1)S(1)}, u32[]{:S(2)}, u32[]{:S(2)}) async-start(bf16[8,64,8,128]{3,2,0,1:T(8,128)(2,1)} %bitcast.5), calls=%async_computation.1 | async-start | bytes 2097152 | tf_op jit(solution)/shard_map/all_to_all | solution.py:54
  58.2 0.0 copy-done.10
  58.2 56.5 %all_gather.7 = bf16[8,8,4096]{2,1,0:T(8,128)(2,1)S(1)} all-gather(bf16[1,8,4096]{2,1,0:T(8,128)(2,1)S(1)} %copy-done.10), channel_id=1, replica_groups=mesh['span'=8,'seq'=64] {'span'}, dimensions={0}, use_global_device_ids=true | all-gather | bytes 589824 | tf_op jit(solution)/shard_map/all_gather | solution.py:51
  114.6 0.1 copy.16
  114.8 0.5 copy-done.12
  115.3 0.6 fusion.83
  115.9 0.0 all-to-all-done.1
  115.9 1.4 broadcast_in_dim.152
  117.3 16.8 %all-to-all-start.2 = ((bf16[8,64,8,128]{3,2,0,1:T(8,128)(2,1)}), bf16[8,64,8,128]{3,2,0,1:T(8,128)(2,1)}, u32[]{:S(2)}, u32[]{:S(2)}) async-start(bf16[8,64,8,128]{3,2,0,1:T(8,128)(2,1)} %bitcast.9), calls=%async_computation.2 | async-start | bytes 2097152 | tf_op jit(solution)/shard_map/all_to_all | solution.py:55
  134.1 0.0 copy-done
  134.1 1.1 fusion.72
  135.2 0.0 copy-start.11
  135.3 0.1 dynamic_slice.3
  135.3 0.6 copy-done.11
  135.9 0.8 fusion.82
  136.7 1.2 fusion.64
  137.9 1.3 fusion.70
  139.3 1.2 fusion.68
  140.5 1.3 fusion.66
  141.7 0.3 fusion.104
  142.1 0.3 fusion.98
  142.4 0.0 copy-done.5
  142.4 0.3 fusion.99
  142.7 1.2 fusion.100
  143.9 1.2 fusion.101
  145.1 1.2 fusion.102
  146.4 1.4 fusion.103
  147.7 1.4 fusion.97
  149.1 0.0 copy-done.8
  149.1 0.2 fusion.16
  149.3 0.0 copy-done.3
  149.4 0.2 fusion.18
  149.6 0.0 copy-done.1
  149.6 0.2 fusion.20
  149.8 0.2 fusion.22
  150.1 0.2 fusion.24
  150.3 0.2 fusion.26
  150.5 0.2 fusion.28
  150.8 0.0 copy-done.6
  150.8 0.2 fusion.30
  151.0 37.9 %all-to-all-done.2 = bf16[8,64,8,128]{3,2,0,1:T(8,128)(2,1)} async-done(((bf16[8,64,8,128]{3,2,0,1:T(8,128)(2,1)}), bf16[8,64,8,128]{3,2,0,1:T(8,128)(2,1)}, u32[]{:S(2)}, u32[]{:S(2)}) %all-to-all-start.2) | async-done | bytes 1048608 | tf_op jit(solution)/shard_map/all_to_all | solution.py:55
  188.9 1.4 fusion.15
  190.3 0.0 copy-start.2
  190.3 1.2 fusion.14
  191.6 0.0 copy-done.2
  191.6 1.2 fusion.13
  192.8 1.2 fusion.12
  194.0 1.2 fusion.11
  195.2 1.2 fusion.10
  196.4 1.2 fusion.9
  197.7 1.3 multiply_reduce_fusion
  199.0 0.1 multiply_convert_fusion
  199.1 24.0 %all_to_all.28 = bf16[64,4,128]{2,1,0:T(4,128)(2,1)S(1)} all-to-all(bf16[64,4,128]{2,1,0:T(4,128)(2,1)S(1)} %bitcast.112), channel_id=1, replica_groups=mesh['span'=8,'seq'=64] {'seq'}, dimensions={0} | all-to-all | bytes 131072 | tf_op jit(solution)/shard_map/all_to_all | solution.py:102
  223.1 0.7 reshape.759
  (16 shorter events, 0.1 us)
Async XLA Ops:
  0.0 134.1 %copy-start = (f32[64,4096]{1,0:T(8,128)S(1)}, f32[64,4096]{1,0:T(8,128)}, u32[]{:S(2)}) copy-start(f32[64,4096]{1,0:T(8,128)} %param.11) | copy-start | bytes 3145732
  1.7 21.9 %copy-start.9 = (bf16[1,8,4096]{2,1,0:T(8,128)(2,1)S(1)}, bf16[1,8,4096]{2,1,0:T(8,128)(2,1)}, u32[]{:S(2)}) copy-start(bf16[1,8,4096]{2,1,0:T(8,128)(2,1)} %param.7) | copy-start | bytes 196612
  1.7 38.8 %all-to-all-start = ((bf16[64,4,128]{2,1,0:T(4,128)(2,1)}), bf16[64,4,128]{2,1,0:T(4,128)(2,1)S(1)}, u32[]{:S(2)}, u32[]{:S(2)}) async-start(bf16[64,4,128]{2,1,0:T(4,128)(2,1)} %copy.14), calls=%async_computation | async-start | bytes 131072 | tf_op jit(solution)/shard_map/all_to_all | solution.py:41
  41.8 16.4 %copy-start.10 = (bf16[1,8,4096]{2,1,0:T(8,128)(2,1)S(1)}, bf16[1,8,4096]{2,1,0:T(8,128)(2,1)}, u32[]{:S(2)}) copy-start(bf16[1,8,4096]{2,1,0:T(8,128)(2,1)} %param.8) | copy-start | bytes 196612
  41.8 74.2 %all-to-all-start.1 = ((bf16[8,64,8,128]{3,2,0,1:T(8,128)(2,1)}), bf16[8,64,8,128]{3,2,0,1:T(8,128)(2,1)S(1)}, u32[]{:S(2)}, u32[]{:S(2)}) async-start(bf16[8,64,8,128]{3,2,0,1:T(8,128)(2,1)} %bitcast.5), calls=%async_computation.1 | async-start | bytes 2097152 | tf_op jit(solution)/shard_map/all_to_all | solution.py:54
  114.6 0.7 copy-start.12
  115.9 26.4 %copy-start.5 = (bf16[8,64,8,128]{3,2,0,1:T(8,128)(2,1)}, bf16[8,64,8,128]{3,2,0,1:T(8,128)(2,1)S(1)}, u32[]{:S(2)}) copy-start(bf16[8,64,8,128]{3,2,0,1:T(8,128)(2,1)S(1)} %all-to-all-done.1) | copy-start | bytes 3145732
  117.3 71.6 %all-to-all-start.2 = ((bf16[8,64,8,128]{3,2,0,1:T(8,128)(2,1)}), bf16[8,64,8,128]{3,2,0,1:T(8,128)(2,1)}, u32[]{:S(2)}, u32[]{:S(2)}) async-start(bf16[8,64,8,128]{3,2,0,1:T(8,128)(2,1)} %bitcast.9), calls=%async_computation.2 | async-start | bytes 2097152 | tf_op jit(solution)/shard_map/all_to_all | solution.py:55
  135.2 0.7 copy-start.11
  142.0 7.1 %copy-start.8 = (f32[256,512]{1,0:T(8,128)}, f32[256,512]{1,0:T(8,128)S(1)}, u32[]{:S(2)}) copy-start(f32[256,512]{1,0:T(8,128)S(1)} %get-tuple-element.45) | copy-start | bytes 1572868
  146.3 3.2 %copy-start.1 = (f32[256,512]{1,0:T(8,128)}, f32[256,512]{1,0:T(8,128)S(1)}, u32[]{:S(2)}) copy-start(f32[256,512]{1,0:T(8,128)S(1)} %get-tuple-element.41) | copy-start | bytes 1572868
  147.7 1.6 copy-start.3
  149.1 1.7 copy-start.6
  188.9 1.4 copy-start.4
  190.3 1.3 copy-start.2
  196.4 1.3 copy-start.7
where the time goes:
time: 225 us; the launch traced here: 224 us
  blocking collectives  97.2 us (43%)
  starting transfers between devices  55 us (24%)
  waiting for transfers between devices  37.9 us (17%)
  matrix products  18.4 us (8%)
  other arithmetic  8.45 us (4%)
  local copies, waits for them, and re-layouts  6.51 us (3%)
    all_gather x1, blocking collectives, body(): lax.all_gather(value_rows, 'span', axis=0, tiled=True)  56.5 us
    all_to_all x1, waiting for transfers between devices, body(): lax.all_to_all(head_layout(all_values), 'seq', split_axis=1, concat_axis=...  37.9 us
    all_to_all x1, blocking collectives, body(): lax.all_to_all(mixed_send, 'seq', split_axis=0, concat_axis=0, tiled=True)  24 us
    all_to_all x1, starting transfers between devices, body(): lax.all_to_all(query_send, 'seq', split_axis=0, concat_axis=0, tiled=True)  21.9 us
    all_to_all x1, starting transfers between devices, body(): lax.all_to_all(head_layout(all_values), 'seq', split_axis=1, concat_axis=...  16.8 us
    all_gather x1, blocking collectives, body(): lax.all_gather(key_rows, 'span', axis=0, tiled=True)  16.7 us
    all_to_all x1, starting transfers between devices, body(): lax.all_to_all(head_layout(all_keys), 'seq', split_axis=1, concat_axis=1,...  16.4 us
    dot_general x8, matrix products, body(): jnp.einsum('hqk,khd->hqd', weights.astype(jnp.bfloat16), value_block, pre...  9.95 us
  transfers between devices with their start and end apart: 3, of which 1 were waited for; matrix products, arithmetic and copies ran while one was open for 8% of the time, Pallas kernels for 0%

commit v1 on v0

v1 whole, which is shorter than its diff:
```python
import functools
import math

import jax
import jax.numpy as jnp
from jax import lax
from jax.experimental import pallas as pl
from jax.experimental.pallas import tpu as pltpu
from jax.sharding import PartitionSpec as P

HEAD_DIM = 128
EPSILON = 1e-5
MASKED = -1e30
LOWEST = -1e4
TINY = 1e-30
MESH = pl.DeviceIdType.MESH


def kernel(
    spans, z_far, side, tok,
    query_ref, key_ref, value_ref, counts_ref, levels_ref, gate_ref, out_ref,
    key_in, query_in, value_in, key_all, query_all, value_all, part, part_in, lse, lse_in,
    mixed, gate_v,
    send_sem, recv_sem, own_sem, key_sems, query_sems, value_sems, part_sems, lse_sems,
    out_send, out_recv, out_own, gate_sem,
):
    column = spans * z_far
    rows = z_far * tok
    span = lax.axis_index("span")
    seq = lax.axis_index("seq")
    z_hi = lax.rem(seq, z_far)
    plane = lax.div(seq, z_far)
    row_y, col_x = lax.div(plane, side), lax.rem(plane, side)
    core = lax.rem(span, 2)
    place = z_hi * spans + span
    key_at = jnp.where(core == 0, row_y, col_x)
    query_at = jnp.where(core == 0, col_x, row_y)
    key_step = jnp.where(core == 0, side, 1)
    query_step = jnp.where(core == 0, 1, side)
    slot = span * z_far + z_hi

    def at_place(other):
        other_hi, other_span = lax.div(other, spans), lax.rem(other, spans)
        return {"span": other_span, "seq": plane * z_far + other_hi}

    def other_place(step):
        half = lax.div(step + 1, 2)
        away = column // 2 + jnp.where(lax.rem(step, 2) == 0, half, -half)
        return lax.rem(place + away, column)

    def key_peer(turn):
        other = lax.rem(key_at + turn, side)
        return other, {"span": span, "seq": seq + (other - key_at) * key_step * z_far}

    def query_peer(turn):
        other = lax.rem(query_at + turn, side)
        return other, {"span": span, "seq": seq + (other - query_at) * query_step * z_far}

    def channels(head):
        return pl.ds(pl.multiple_of(head * HEAD_DIM, HEAD_DIM), HEAD_DIM)

    pairs = ((key_ref, key_in, 0), (query_ref, query_in, 1), (value_ref, value_in, 2))

    barrier = pltpu.get_barrier_semaphore()

    def greet(step, carry):
        pl.semaphore_signal(barrier, inc=1, device_id=at_place(other_place(step)), device_id_type=MESH)
        return carry

    lax.fori_loop(0, column - 1, greet, 0)
    for turn in range(1, side):
        pl.semaphore_signal(barrier, inc=1, device_id=key_peer(turn)[1], device_id_type=MESH)
        pl.semaphore_signal(barrier, inc=1, device_id=query_peer(turn)[1], device_id_type=MESH)

    gate_copy = pltpu.make_async_copy(gate_ref.at[:, channels(place)], gate_v, gate_sem)
    gate_copy.start()
    own = []
    for source, target, n in pairs:
        copy = pltpu.make_async_copy(source.at[0, :, channels(place)], target.at[slot], own_sem.at[n])
        copy.start()
        own.append(copy)
    pl.semaphore_wait(barrier, column - 1 + 2 * (side - 1))

    for source, target, n in pairs:
        def spread(step, carry, source=source, target=target, n=n):
            other = other_place(step)
            pltpu.make_async_remote_copy(
                src_ref=source.at[0, :, channels(other)], dst_ref=target.at[slot],
                send_sem=send_sem.at[n], recv_sem=recv_sem.at[n],
                device_id=at_place(other), device_id_type=MESH,
            ).start()
            return carry
        lax.fori_loop(0, column - 1, spread, 0)

    def arrived(target, n):
        own[n].wait()
        rest = target.at[pl.ds(0, column - 1)]
        pltpu.make_async_copy(rest, rest, recv_sem.at[n]).wait()
        whole = target[...].astype(jnp.float32).reshape(spans, rows, HEAD_DIM)
        return whole.astype(jnp.bfloat16)

    def gather(block, target, sems, peer, here):
        target[:, here] = block
        copies = []
        for turn in range(1, side):
            copy = pltpu.make_async_remote_copy(
                src_ref=target.at[:, here], dst_ref=target.at[:, here],
                send_sem=sems.at[0, turn], recv_sem=sems.at[1, turn],
                device_id=peer(turn)[1], device_id_type=MESH,
            )
            copy.start()
            copies.append(copy)
        return copies

    key_copies = gather(arrived(key_in, 0), key_all, key_sems, key_peer, key_at)
    query_copies = gather(arrived(query_in, 1), query_all, query_sems, query_peer, query_at)
    value_copies = gather(arrived(value_in, 2), value_all, value_sems, key_peer, key_at)
    for copy in key_copies + query_copies + value_copies:
        copy.wait()

    many = side * rows
    lanes = lax.broadcasted_iota(jnp.int32, (1, many), 1)
    position = (plane + (lax.div(lanes, rows) - key_at) * key_step) * rows + lax.rem(lanes, rows)
    bias = jnp.concatenate(
        [jnp.where(position < counts_ref[c], 0.0, MASKED) for c in range(spans)], axis=1
    )
    diagonal = lax.broadcasted_iota(jnp.int32, (many, many), 0) == lax.broadcasted_iota(
        jnp.int32, (many, many), 1
    )
    factor = math.log2(math.e) / math.sqrt(HEAD_DIM)
    for i in range(spans):
        wide = (i + 1) * many
        queries = query_all[i].reshape(many, HEAD_DIM)
        keys = key_all[0 : i + 1].reshape(wide, HEAD_DIM)
        values = value_all[0 : i + 1].reshape(wide, HEAD_DIM)
        scores = lax.dot_general(
            queries, keys, (((1,), (1,)), ((), ())), preferred_element_type=jnp.float32
        )
        scores = scores * factor + bias[:, :wide]
        top = jnp.maximum(jnp.max(scores, axis=1, keepdims=True), LOWEST)
        weights = jnp.exp2(scores - top)
        total = jnp.maximum(jnp.sum(weights, axis=1, keepdims=True), TINY)
        mix = jnp.dot(weights.astype(jnp.bfloat16), values, preferred_element_type=jnp.float32)
        part[:, i] = (mix / total).astype(jnp.bfloat16).reshape(side, rows, HEAD_DIM)
        column_lse = top + jnp.log2(total)
        lse[i : i + 1, :] = jnp.sum(jnp.where(diagonal, column_lse, 0.0), axis=0, keepdims=True)

    copies = []
    for turn in range(1, side):
        other, peer = query_peer(turn)
        for source, target, sems in (
            (part.at[other], part_in.at[turn - 1], part_sems),
            (lse, lse_in.at[turn - 1], lse_sems),
        ):
            copy = pltpu.make_async_remote_copy(
                src_ref=source, dst_ref=target, send_sem=sems.at[0, turn], recv_sem=sems.at[1, turn],
                device_id=peer, device_id_type=MESH,
            )
            copy.start()
            copies.append(copy)
    gate_copy.wait()
    for copy in copies:
        copy.wait()

    tables = [lse[...]] + [lse_in[n] for n in range(side - 1)]
    top = functools.reduce(jnp.maximum, tables)
    tables = [jnp.exp2(table - top) for table in tables]
    total = functools.reduce(jnp.add, tables)
    tables = [table / total for table in tables]
    mine = lax.broadcasted_iota(jnp.int32, (rows, many), 1) == (
        query_at * rows + lax.broadcasted_iota(jnp.int32, (rows, many), 0)
    )
    for i in range(spans):
        attended = jnp.zeros((rows, HEAD_DIM), jnp.float32)
        for n in range(side):
            block = part[query_at, i] if n == 0 else part_in[n - 1, i]
            share = jnp.sum(jnp.where(mine, tables[n][i : i + 1], 0.0), axis=1, keepdims=True)
            attended = attended + share * block.astype(jnp.float32)
        mean = jnp.mean(attended * attended, axis=1, keepdims=True)
        gate = gate_v[pl.ds(levels_ref[i], 1), :]
        normed = attended * lax.rsqrt(mean + EPSILON) * gate
        mixed[i * z_far : (i + 1) * z_far] = normed.reshape(z_far, tok, HEAD_DIM).astype(jnp.bfloat16)

    back = pltpu.make_async_copy(mixed.at[slot], out_ref.at[0, :, channels(place)], out_own)
    back.start()

    def send_back(step, carry):
        other = other_place(step)
        other_slot = lax.rem(other, spans) * z_far + lax.div(other, spans)
        pltpu.make_async_remote_copy(
            src_ref=mixed.at[other_slot], dst_ref=out_ref.at[0, :, channels(place)],
            send_sem=out_send, recv_sem=out_recv, device_id=at_place(other), device_id_type=MESH,
        ).start()
        return carry

    lax.fori_loop(0, column - 1, send_back, 0)
    for n in range(3):
        rest = key_in.at[pl.ds(0, column - 1)]
        pltpu.make_async_copy(rest, rest, send_sem.at[n]).wait()
    rest = mixed.at[pl.ds(0, column - 1)]
    pltpu.make_async_copy(rest, rest, out_send).wait()
    back.wait()
    rest = out_ref.at[0, :, pl.ds(0, (column - 1) * HEAD_DIM)]
    pltpu.make_async_copy(rest, rest, out_recv).wait()


def body(query_rows, key_rows, value_rows, counts, levels, gate_table):
    spans = lax.axis_size("span")
    seq_size = lax.axis_size("seq")
    tok, width = query_rows.shape[1:]
    column = width // HEAD_DIM
    z_far = column // spans
    side = math.isqrt(seq_size // z_far)
    rows = z_far * tok
    bf16, f32 = jnp.bfloat16, jnp.float32
    landing = pltpu.VMEM((column, tok, HEAD_DIM), bf16)
    gathered = pltpu.VMEM((spans, side, rows, HEAD_DIM), bf16)
    dma = pltpu.SemaphoreType.DMA
    anywhere = pl.BlockSpec(memory_space=pl.ANY)
    scalars = pl.BlockSpec(memory_space=pltpu.SMEM)
    return pl.pallas_call(
        functools.partial(kernel, spans, z_far, side, tok),
        out_shape=jax.ShapeDtypeStruct(query_rows.shape, bf16),
        in_specs=[anywhere, anywhere, anywhere, scalars, scalars, anywhere],
        out_specs=anywhere,
        scratch_shapes=[
            landing, landing, landing, gathered, gathered, gathered,
            pltpu.VMEM((side, spans, rows, HEAD_DIM), bf16),
            pltpu.VMEM((side - 1, spans, rows, HEAD_DIM), bf16),
            pltpu.VMEM((spans, side * rows), f32),
            pltpu.VMEM((side - 1, spans, side * rows), f32),
            landing,
            pltpu.VMEM((gate_table.shape[0], HEAD_DIM), f32),
            dma((3,)), dma((3,)), dma((3,)),
            dma((2, side)), dma((2, side)), dma((2, side)), dma((2, side)), dma((2, side)),
            dma, dma, dma, dma,
        ],
        compiler_params=pltpu.CompilerParams(
            collective_id=0, has_side_effects=True, vmem_limit_bytes=32 * 1024 * 1024
        ),
        cost_estimate=pl.CostEstimate(
            flops=600_000_000, bytes_accessed=1_000_000, transcendentals=600_000
        ),
    )(query_rows, key_rows, value_rows, counts, levels, gate_table)


def solution(mesh):
    placed = (P("span", "seq", None), P("span", "seq", None), P("span", "seq", None), P(), P(), P())
    return jax.shard_map(
        body, mesh=mesh, in_specs=placed, out_specs=P("span", "seq", None), check_vma=False
    )
```

time: 225 us -> 57.2 us (0.25)
  blocking collectives: 97.2 us -> 0 us
  starting transfers between devices: 55 us -> 0 us
  Pallas kernels: 0 us -> 51.2 us
  waiting for transfers between devices: 37.9 us -> 0 us
  matrix products: 18.4 us -> 0 us
  other arithmetic: 8.45 us -> 0 us
    all_gather x2 -> x0, blocking collectives: 73.2 us -> none  [the longest x1 56.5 us: body(): lax.all_gather(value_rows, 'span', axis=0, tiled=True)]
    all_to_all x3 -> x0, starting transfers between devices: 55 us -> none  [the longest x1 21.9 us: body(): lax.all_to_all(query_send, 'seq', split_axis=0, concat_axis=0, tiled=True)]
    pallas_call x0 -> x1, Pallas kernels: none -> 51.2 us  [body(): pl.pallas_call(functools.partial(kernel, spans, z_far, side, tok), out_sh...]
    all_to_all x3 -> x0, waiting for transfers between devices: 37.9 us -> none  [the longest x1 37.9 us: body(): lax.all_to_all(head_layout(all_values), 'seq', split_axis=1, concat_axis=...]
    all_to_all x1 -> x0, blocking collectives: 24 us -> none  [body(): lax.all_to_all(mixed_send, 'seq', split_axis=0, concat_axis=0, tiled=True)]
    dot_general x17 -> x0, matrix products: 18.4 us -> none  [the longest x8 9.95 us: body(): jnp.einsum('hqk,khd->hqd', weights.astype(jnp.bfloat16), value_block, pre...]
    and x4 -> x0, other arithmetic: 4.98 us -> none  [body(): allowed = (span_id <= my_span) & (positions < pick_entry(counts, span_id))]
    unnamed x27 -> x13, local copies, waits for them, and re-layouts: 2.07 us -> 5.68 us
  transfers between devices with their start and end apart: 3 -> 0, of which waited for: 1 -> 0; matrix products, arithmetic and copies ran while one was open for 8% -> 0% of each run, Pallas kernels for 0% -> 0%
where the time goes in v1:
time: 57.2 us; the launch traced here: 56.9 us
  Pallas kernels  51.2 us (90%)
  local copies, waits for them, and re-layouts  5.68 us (10%)
    pallas_call x1, Pallas kernels, body(): pl.pallas_call(functools.partial(kernel, spans, z_far, side, tok), out_sh...  51.2 us
    unnamed x13, local copies, waits for them, and re-layouts  5.68 us

profile of v1, /device:TPU:1, one launch (start us, length us, event | category | flops | bytes accessed | tf_op | source)
XLA Modules:
  0.0 56.9 jit_solution(14688106617885221426)
XLA Ops:
  0.0 0.0 copy-start
  0.0 1.2 %copy-done = f32[64,4096]{1,0:T(8,128)S(1)} copy-done((f32[64,4096]{1,0:T(8,128)S(1)}, f32[64,4096]{1,0:T(8,128)}, u32[]{:S(2)}) %copy-start) | copy-done | bytes 1048600
  1.2 0.0 copy-start.1
  1.2 0.8 %copy-done.1 = bf16[1,8,4096]{2,1,0:T(8,128)(2,1)S(1)} copy-done((bf16[1,8,4096]{2,1,0:T(8,128)(2,1)S(1)}, bf16[1,8,4096]{2,1,0:T(8,128)(2,1)}, u32[]{:S(2)}) %copy-start.1) | copy-done | bytes 65560
  2.1 0.0 copy-start.2
  2.1 0.8 %copy-done.2 = bf16[1,8,4096]{2,1,0:T(8,128)(2,1)S(1)} copy-done((bf16[1,8,4096]{2,1,0:T(8,128)(2,1)S(1)}, bf16[1,8,4096]{2,1,0:T(8,128)(2,1)}, u32[]{:S(2)}) %copy-start.2) | copy-done | bytes 65560
  2.9 0.0 copy-start.3
  2.9 0.8 %copy-done.3 = bf16[1,8,4096]{2,1,0:T(8,128)(2,1)S(1)} copy-done((bf16[1,8,4096]{2,1,0:T(8,128)(2,1)S(1)}, bf16[1,8,4096]{2,1,0:T(8,128)(2,1)}, u32[]{:S(2)}) %copy-start.3) | copy-done | bytes 65560
  3.7 0.0 copy-start.4
  3.7 0.7 %copy-done.4 = s32[8]{0:T(128)S(1)} copy-done((s32[8]{0:T(128)S(1)}, s32[8]{0:T(128)}, u32[]{:S(2)}) %copy-start.4) | copy-done | bytes 56
  4.4 0.0 copy-start.5
  4.4 0.7 %copy-done.5 = s32[8]{0:T(128)S(1)} copy-done((s32[8]{0:T(128)S(1)}, s32[8]{0:T(128)}, u32[]{:S(2)}) %copy-start.5) | copy-done | bytes 56
  5.1 51.2 %shard_map.64 = bf16[1,8,4096]{2,1,0:T(8,128)(2,1)S(1)} custom-call(bf16[1,8,4096]{2,1,0:T(8,128)(2,1)S(1)} %copy-done.1, bf16[1,8,4096]{2,1,0:T(8,128)(2,1)S(1)} %copy-done.2, bf16[1,8,4096]{2,1,0:T(8,128)(2,1)S(1)} %copy-done.3, s32[8]{0:T(128)S(1)} %copy-done.4, s32[8]{0:T(128)S(1)} %copy-done.5, f32[64,4096]{1,0:T(8,128)S(1)} %copy-done), custom_call_target="tpu_custom_call" | custom-call | flops 600000000 | bytes 1000000 | tf_op jit(solution)/shard_map/pallas_call | solution.py:221
  56.2 0.6 %copy.8 = bf16[1,8,4096]{2,1,0:T(8,128)(2,1)} copy(bf16[1,8,4096]{2,1,0:T(8,128)(2,1)S(1)} %shard_map.64) | data formatting | bytes 131072
Async XLA Ops:
  0.0 1.2 %copy-start = (f32[64,4096]{1,0:T(8,128)S(1)}, f32[64,4096]{1,0:T(8,128)}, u32[]{:S(2)}) copy-start(f32[64,4096]{1,0:T(8,128)} %gate_ref.1) | copy-start | bytes 3145732
  1.2 0.8 %copy-start.1 = (bf16[1,8,4096]{2,1,0:T(8,128)(2,1)S(1)}, bf16[1,8,4096]{2,1,0:T(8,128)(2,1)}, u32[]{:S(2)}) copy-start(bf16[1,8,4096]{2,1,0:T(8,128)(2,1)} %query_ref.1) | copy-start | bytes 196612
  2.1 0.8 %copy-start.2 = (bf16[1,8,4096]{2,1,0:T(8,128)(2,1)S(1)}, bf16[1,8,4096]{2,1,0:T(8,128)(2,1)}, u32[]{:S(2)}) copy-start(bf16[1,8,4096]{2,1,0:T(8,128)(2,1)} %key_ref.1) | copy-start | bytes 196612
  2.9 0.8 %copy-start.3 = (bf16[1,8,4096]{2,1,0:T(8,128)(2,1)S(1)}, bf16[1,8,4096]{2,1,0:T(8,128)(2,1)}, u32[]{:S(2)}) copy-start(bf16[1,8,4096]{2,1,0:T(8,128)(2,1)} %value_ref.1) | copy-start | bytes 196612
  3.7 0.7 %copy-start.4 = (s32[8]{0:T(128)S(1)}, s32[8]{0:T(128)}, u32[]{:S(2)}) copy-start(s32[8]{0:T(128)} %counts_ref.1) | copy-start | bytes 100
  4.4 0.7 %copy-start.5 = (s32[8]{0:T(128)S(1)}, s32[8]{0:T(128)}, u32[]{:S(2)}) copy-start(s32[8]{0:T(128)} %levels_ref.1) | copy-start | bytes 100

commit v2 on v1

v2 whole, which is shorter than its diff:
```python
import functools
import math

import jax
import jax.numpy as jnp
from jax import lax
from jax.experimental import pallas as pl
from jax.experimental.pallas import tpu as pltpu
from jax.sharding import PartitionSpec as P

HEAD_DIM = 128
EPSILON = 1e-5
MASKED = -1e30
LOWEST = -1e4
TINY = 1e-30
MESH = pl.DeviceIdType.MESH
VMEM_BYTES = 32 * 1024 * 1024


def kernel(
    spans, z_far, side, tok,
    query_ref, key_ref, value_ref, counts_ref, levels_ref, gate_ref, out_ref,
    key_all, query_all, value_all, keys_flat, values_flat, chances, part, part_in, lse, lse_in,
    mixed, gate_v, counts_s, levels_s,
    send_sem, recv_sem, key_sems, query_sems, value_sems, part_sems, lse_sems,
    out_send, out_recv, small_sems,
):
    column = spans * z_far
    half_size = column // 2
    near = z_far // 2
    rows = z_far * tok
    many = side * rows
    pairs = spans // 2
    span = lax.axis_index("span")
    seq = lax.axis_index("seq")
    z_hi = lax.rem(seq, z_far)
    plane = lax.div(seq, z_far)
    row_y, col_x = lax.div(plane, side), lax.rem(plane, side)
    core = lax.rem(span, 2)
    place = z_hi * spans + span
    key_at = jnp.where(core == 0, row_y, col_x)
    query_at = jnp.where(core == 0, col_x, row_y)
    key_step = jnp.where(core == 0, side, 1)
    query_step = jnp.where(core == 0, 1, side)
    my_half = lax.div(place, half_size)

    def at_place(other):
        return {"span": lax.rem(other, spans), "seq": plane * z_far + lax.div(other, spans)}

    def other_place(step):
        half = lax.div(step + 1, 2)
        away = column // 2 + jnp.where(lax.rem(step, 2) == 0, half, -half)
        return lax.rem(place + away, column)

    def key_peer(turn):
        other = lax.rem(key_at + turn, side)
        return {"span": span, "seq": seq + (other - key_at) * key_step * z_far}

    def query_peer(turn):
        other = lax.rem(query_at + turn, side)
        return {"span": span, "seq": seq + (other - query_at) * query_step * z_far}

    def channels(head):
        return pl.ds(pl.multiple_of(head * HEAD_DIM, HEAD_DIM), HEAD_DIM)

    barrier = pltpu.get_barrier_semaphore()

    def greet(step, carry):
        pl.semaphore_signal(barrier, inc=1, device_id=at_place(other_place(step)), device_id_type=MESH)
        return carry

    lax.fori_loop(0, column - 1, greet, 0)
    for turn in range(1, side):
        pl.semaphore_signal(barrier, inc=1, device_id=key_peer(turn), device_id_type=MESH)
        pl.semaphore_signal(barrier, inc=1, device_id=query_peer(turn), device_id_type=MESH)

    arrays = ((key_ref, key_all, 0), (query_ref, query_all, 1), (value_ref, value_all, 2))
    for source, target, n in arrays:
        here = query_at if n == 1 else key_at
        pltpu.make_async_copy(
            source.at[0, :, channels(place)], target.at[here, z_hi, span], recv_sem.at[n, my_half]
        ).start()
    small = [
        pltpu.make_async_copy(counts_ref, counts_s, small_sems.at[0]),
        pltpu.make_async_copy(levels_ref, levels_s, small_sems.at[1]),
        pltpu.make_async_copy(gate_ref.at[:, channels(place)], gate_v, small_sems.at[2]),
    ]
    for copy in small:
        copy.start()
    pl.semaphore_wait(barrier, column - 1 + 2 * (side - 1))

    for source, target, n in arrays:
        def spread(step, carry, source=source, target=target, n=n):
            other = other_place(step)
            along = lax.rem(other, 2) == 0
            there = jnp.where(along, col_x, row_y) if n == 1 else jnp.where(along, row_y, col_x)
            pltpu.make_async_remote_copy(
                src_ref=source.at[0, :, channels(other)], dst_ref=target.at[there, z_hi, span],
                send_sem=send_sem.at[n], recv_sem=recv_sem.at[n, my_half],
                device_id=at_place(other), device_id_type=MESH,
            ).start()
            return carry
        lax.fori_loop(0, column - 1, spread, 0)

    def gather(n, half):
        target = arrays[n][1]
        here, peer = (query_at, query_peer) if n == 1 else (key_at, key_peer)
        sems = (key_sems, query_sems, value_sems)[n]
        block = target.at[here, pl.ds(half * near, near)]
        pltpu.make_async_copy(block, block, recv_sem.at[n, half]).wait()
        copies = []
        for turn in range(1, side):
            copy = pltpu.make_async_remote_copy(
                src_ref=block, dst_ref=block, send_sem=sems.at[0, half, turn],
                recv_sem=sems.at[1, half, turn], device_id=peer(turn), device_id_type=MESH,
            )
            copy.start()
            copies.append(copy)
        return copies

    sent = []
    scoring = gather(0, 1) + gather(1, 1) + gather(0, 0) + gather(1, 0)
    mixing = gather(2, 1) + gather(2, 0)
    sent += scoring + mixing

    lanes = lax.broadcasted_iota(jnp.int32, (1, many), 1)
    position = (plane + (lax.div(lanes, rows) - key_at) * key_step) * rows + lax.rem(lanes, rows)
    for copy in small:
        copy.wait()
    bias = jnp.concatenate(
        [jnp.where(position < counts_s[c], 0.0, MASKED) for c in range(spans)], axis=1
    )
    row_ids = lax.broadcasted_iota(jnp.int32, (many, many), 0)
    diagonal = row_ids == lax.broadcasted_iota(jnp.int32, (many, many), 1)
    later = jnp.where(lax.rem(lax.div(row_ids, tok), 2) == 0, MASKED, 0.0)
    factor = math.log2(math.e) / math.sqrt(HEAD_DIM)

    for copy in scoring:
        copy.wait_recv()

    def flat(tiles):
        wide = tiles.astype(jnp.float32)
        return wide.reshape(math.prod(wide.shape[:-1]), HEAD_DIM).astype(jnp.bfloat16)

    def flatten(source, target):
        for c in range(spans):
            target[c * many : (c + 1) * many] = flat(source[:, :, c])

    def score(half):
        totals = []
        for j in range(pairs):
            wide = 2 * (j + 1) * many
            queries = flat(query_all[:, half * near : (half + 1) * near, 2 * j : 2 * j + 2])
            scores = lax.dot_general(
                queries, keys_flat[:wide], (((1,), (1,)), ((), ())),
                preferred_element_type=jnp.float32,
            )
            scores = scores * factor + bias[:, :wide]
            scores = jnp.concatenate([scores[:, : wide - many], scores[:, wide - many :] + later], axis=1)
            top = jnp.maximum(jnp.max(scores, axis=1, keepdims=True), LOWEST)
            weights = jnp.exp2(scores - top)
            total = jnp.maximum(jnp.sum(weights, axis=1, keepdims=True), TINY)
            chances[half, j, :, :wide] = weights.astype(jnp.bfloat16)
            both = jnp.sum(jnp.where(diagonal, top + jnp.log2(total), 0.0), axis=0, keepdims=True)
            lse[half, j : j + 1, :] = both
            lse[half, pairs + j : pairs + j + 1, :] = both
            totals.append(1.0 / total)
        return totals

    def mix(half, totals):
        for j in range(pairs):
            wide = 2 * (j + 1) * many
            mixture = jnp.dot(
                chances[half, j, :, :wide], values_flat[:wide], preferred_element_type=jnp.float32
            )
            mixture = (mixture * totals[j]).reshape(side, near, 2, tok, HEAD_DIM)
            part[half, :, :, 2 * j : 2 * j + 2] = mixture.astype(jnp.bfloat16)
        copies = []
        for turn in range(1, side):
            other = lax.rem(query_at + turn, side)
            for source, target, sems in (
                (part.at[half, other], part_in.at[half, turn - 1], part_sems),
                (lse.at[half], lse_in.at[half, turn - 1], lse_sems),
            ):
                copy = pltpu.make_async_remote_copy(
                    src_ref=source, dst_ref=target, send_sem=sems.at[0, half, turn],
                    recv_sem=sems.at[1, half, turn], device_id=query_peer(turn), device_id_type=MESH,
                )
                copy.start()
                copies.append(copy)
        return copies

    flatten(key_all, keys_flat)
    totals = [score(0), score(1)]
    for copy in mixing:
        copy.wait_recv()
    flatten(value_all, values_flat)
    parts = [mix(0, totals[0]), mix(1, totals[1])]
    sent += parts[0] + parts[1]

    cut = 2 * near * tok
    mine = lax.broadcasted_iota(jnp.int32, (cut, many), 1) == (
        query_at * cut + lax.broadcasted_iota(jnp.int32, (cut, many), 0)
    )
    second = lax.rem(lax.div(lax.broadcasted_iota(jnp.int32, (cut, 1), 0), tok), 2) == 1

    def finish(half):
        for copy in parts[half]:
            copy.wait_recv()
        tables = [lse[half]] + [lse_in[half, n] for n in range(side - 1)]
        top = functools.reduce(jnp.maximum, tables)
        tables = [jnp.exp2(table - top) for table in tables]
        total = functools.reduce(jnp.add, tables)
        tables = [table / total for table in tables]
        for j in range(pairs):
            pick = slice(2 * j, 2 * j + 2)
            attended = jnp.zeros((cut, HEAD_DIM), jnp.float32)
            for n in range(side):
                tile = part[half, query_at, :, pick] if n == 0 else part_in[half, n - 1, :, pick]
                share = jnp.sum(jnp.where(mine, tables[n][j : j + 1], 0.0), axis=1, keepdims=True)
                attended = attended + share * tile.astype(jnp.float32).reshape(cut, HEAD_DIM)
            mean = jnp.mean(attended * attended, axis=1, keepdims=True)
            gate = jnp.where(
                second,
                gate_v[pl.ds(levels_s[2 * j + 1], 1), :],
                gate_v[pl.ds(levels_s[2 * j], 1), :],
            )
            normed = attended * lax.rsqrt(mean + EPSILON) * gate
            mixed[half * near : (half + 1) * near, pick] = normed.reshape(
                near, 2, tok, HEAD_DIM
            ).astype(jnp.bfloat16)

        def send_back(step, carry):
            away = half_size // 2 + jnp.where(
                lax.rem(step, 2) == 0, lax.div(step + 1, 2), -lax.div(step + 1, 2)
            )
            other = half * half_size + lax.rem(place + away + half_size, half_size)

            @pl.when(other != place)
            def _():
                pltpu.make_async_remote_copy(
                    src_ref=mixed.at[lax.div(other, spans), lax.rem(other, spans)],
                    dst_ref=out_ref.at[0, :, channels(place)],
                    send_sem=out_send, recv_sem=out_recv,
                    device_id=at_place(other), device_id_type=MESH,
                ).start()

            @pl.when(other == place)
            def _():
                pltpu.make_async_copy(
                    mixed.at[z_hi, span], out_ref.at[0, :, channels(place)], out_recv
                ).start()

            return carry

        lax.fori_loop(0, half_size, send_back, 0)

    finish(0)
    finish(1)
    for source, target, n in arrays:
        rest = source.at[0, :, pl.ds(0, (column - 1) * HEAD_DIM)]
        pltpu.make_async_copy(rest, rest, send_sem.at[n]).wait()
    for copy in sent:
        copy.wait_send()
    rest = out_ref.at[0, :, pl.ds(0, (column - 1) * HEAD_DIM)]
    pltpu.make_async_copy(rest, rest, out_send).wait()
    pltpu.make_async_copy(out_ref, out_ref, out_recv).wait()


def body(query_rows, key_rows, value_rows, counts, levels, gate_table):
    spans = lax.axis_size("span")
    seq_size = lax.axis_size("seq")
    tok, width = query_rows.shape[1:]
    column = width // HEAD_DIM
    z_far = column // spans
    side = math.isqrt(seq_size // z_far)
    many = side * z_far * tok
    pairs = spans // 2
    bf16, f32 = jnp.bfloat16, jnp.float32
    gathered = pltpu.VMEM((side, z_far, spans, tok, HEAD_DIM), bf16)
    flat = pltpu.VMEM((spans * many, HEAD_DIM), bf16)
    dma = pltpu.SemaphoreType.DMA
    hbm = pl.BlockSpec(memory_space=pltpu.HBM)
    return pl.pallas_call(
        functools.partial(kernel, spans, z_far, side, tok),
        out_shape=jax.ShapeDtypeStruct(query_rows.shape, bf16),
        in_specs=[hbm] * 6,
        out_specs=pl.BlockSpec(memory_space=pl.ANY),
        scratch_shapes=[
            gathered, gathered, gathered, flat, flat,
            pltpu.VMEM((2, pairs, many, spans * many), bf16),
            pltpu.VMEM((2, side, z_far // 2, spans, tok, HEAD_DIM), bf16),
            pltpu.VMEM((2, side - 1, z_far // 2, spans, tok, HEAD_DIM), bf16),
            pltpu.VMEM((2, 2 * pairs, many), f32),
            pltpu.VMEM((2, side - 1, 2 * pairs, many), f32),
            pltpu.VMEM((z_far, spans, tok, HEAD_DIM), bf16),
            pltpu.VMEM((gate_table.shape[0], HEAD_DIM), f32),
            pltpu.SMEM(counts.shape, jnp.int32),
            pltpu.SMEM(levels.shape, jnp.int32),
            dma((3,)), dma((3, 2)),
            dma((2, 2, side)), dma((2, 2, side)), dma((2, 2, side)),
            dma((2, 2, side)), dma((2, 2, side)),
            dma, dma, dma((3,)),
        ],
        compiler_params=pltpu.CompilerParams(
            collective_id=0, has_side_effects=True, vmem_limit_bytes=VMEM_BYTES
        ),
        cost_estimate=pl.CostEstimate(
            flops=600_000_000, bytes_accessed=1_000_000, transcendentals=700_000
        ),
    )(*[
        pltpu.with_memory_space_constraint(array, pltpu.HBM)
        for array in (query_rows, key_rows, value_rows, counts, levels, gate_table)
    ])


def solution(mesh):
    placed = (P("span", "seq", None), P("span", "seq", None), P("span", "seq", None), P(), P(), P())
    return jax.shard_map(
        body, mesh=mesh, in_specs=placed, out_specs=P("span", "seq", None), check_vma=False
    )
```

time: 57.2 us -> 49 us (0.86)
  local copies, waits for them, and re-layouts: 5.68 us -> 0.63 us
  Pallas kernels: 51.2 us -> 48.3 us
    unnamed x13 -> x1, local copies, waits for them, and re-layouts: 5.68 us -> 0.63 us
    pallas_call x1, Pallas kernels: 51.2 us -> 48.3 us  [body(): pl.pallas_call(functools.partial(kernel, spans, z_far, side, tok), out_sh...]
where the time goes in v2:
time: 49 us; the launch traced here: 48.9 us
  Pallas kernels  48.3 us (99%)
  local copies, waits for them, and re-layouts  0.63 us (1%)
    pallas_call x1, Pallas kernels, body(): pl.pallas_call(functools.partial(kernel, spans, z_far, side, tok), out_sh...  48.3 us

profile of v2, /device:TPU:1, one launch (start us, length us, event | category | flops | bytes accessed | tf_op | source)
XLA Modules:
  0.0 48.9 jit_solution(5775034990548418565)
XLA Ops:
  0.0 48.3 %shard_map.64 = bf16[1,8,4096]{2,1,0:T(8,128)(2,1)S(1)} custom-call(bf16[1,8,4096]{2,1,0:T(8,128)(2,1)} %query_ref.1, bf16[1,8,4096]{2,1,0:T(8,128)(2,1)} %key_ref.1, bf16[1,8,4096]{2,1,0:T(8,128)(2,1)} %value_ref.1, s32[8]{0:T(128)} %counts_ref.1, s32[8]{0:T(128)} %levels_ref.1, f32[64,4096]{1,0:T(8,128)} %gate_ref.1), custom_call_target="tpu_custom_call" | custom-call | flops 600000000 | bytes 1000000 | tf_op jit(solution)/shard_map/pallas_call | solution.py:284
  48.3 0.6 %copy.8 = bf16[1,8,4096]{2,1,0:T(8,128)(2,1)} copy(bf16[1,8,4096]{2,1,0:T(8,128)(2,1)S(1)} %shard_map.64) | data formatting | bytes 131072

commit v3 on v2

v3 whole, which is shorter than its diff:
```python
import functools
import math

import jax
import jax.numpy as jnp
from jax import lax
from jax.experimental import pallas as pl
from jax.experimental.pallas import tpu as pltpu
from jax.sharding import PartitionSpec as P

HEAD_DIM = 128
EPSILON = 1e-5
MASKED = -1e30
LOWEST = -1e4
TINY = 1e-30
MESH = pl.DeviceIdType.MESH
VMEM_BYTES = 32 * 1024 * 1024


def kernel(
    spans, z_far, side, tok,
    query_ref, key_ref, value_ref, counts_ref, levels_ref, gate_ref, out_ref,
    key_all, query_all, value_all, keys_flat, values_flat, chances, summed, part, part_in, lse, lse_in,
    mixed, gate_v, counts_s, levels_s,
    send_sem, recv_sem, key_sems, query_sems, value_sems, part_sems, lse_sems,
    out_send, out_recv, small_sems,
):
    column = spans * z_far
    half_size = column // 2
    near = z_far // 2
    rows = z_far * tok
    many = side * rows
    pairs = spans // 2
    span = lax.axis_index("span")
    seq = lax.axis_index("seq")
    z_hi = lax.rem(seq, z_far)
    plane = lax.div(seq, z_far)
    row_y, col_x = lax.div(plane, side), lax.rem(plane, side)
    core = lax.rem(span, 2)
    place = z_hi * spans + span
    key_at = jnp.where(core == 0, row_y, col_x)
    query_at = jnp.where(core == 0, col_x, row_y)
    key_step = jnp.where(core == 0, side, 1)
    query_step = jnp.where(core == 0, 1, side)
    my_half = lax.div(place, half_size)

    def at_place(other):
        return {"span": lax.rem(other, spans), "seq": plane * z_far + lax.div(other, spans)}

    def other_place(step):
        half = lax.div(step + 1, 2)
        away = column // 2 + jnp.where(lax.rem(step, 2) == 0, half, -half)
        return lax.rem(place + away, column)

    def key_peer(turn):
        other = lax.rem(key_at + turn, side)
        return {"span": span, "seq": seq + (other - key_at) * key_step * z_far}

    def query_peer(turn):
        other = lax.rem(query_at + turn, side)
        return {"span": span, "seq": seq + (other - query_at) * query_step * z_far}

    def channels(head):
        return pl.ds(pl.multiple_of(head * HEAD_DIM, HEAD_DIM), HEAD_DIM)

    barrier = pltpu.get_barrier_semaphore()

    def greet(step, carry):
        pl.semaphore_signal(barrier, inc=1, device_id=at_place(other_place(step)), device_id_type=MESH)
        return carry

    lax.fori_loop(0, column - 1, greet, 0)
    for turn in range(1, side):
        pl.semaphore_signal(barrier, inc=1, device_id=key_peer(turn), device_id_type=MESH)
        pl.semaphore_signal(barrier, inc=1, device_id=query_peer(turn), device_id_type=MESH)

    arrays = ((key_ref, key_all, 0), (query_ref, query_all, 1), (value_ref, value_all, 2))
    for source, target, n in arrays:
        here = query_at if n == 1 else key_at
        pltpu.make_async_copy(
            source.at[0, :, channels(place)], target.at[here, z_hi, span], recv_sem.at[n, my_half]
        ).start()
    small = [
        pltpu.make_async_copy(counts_ref, counts_s, small_sems.at[0]),
        pltpu.make_async_copy(levels_ref, levels_s, small_sems.at[1]),
        pltpu.make_async_copy(gate_ref.at[:, channels(place)], gate_v, small_sems.at[2]),
    ]
    for copy in small:
        copy.start()
    pl.semaphore_wait(barrier, column - 1 + 2 * (side - 1))

    def zigzag(step):
        half = lax.div(step + 1, 2)
        return jnp.where(lax.rem(step, 2) == 0, half, -half)

    for half in (1, 0):
        first = jnp.where(my_half == half, half_size // 2, 0) + half_size
        for source, target, n in arrays:
            def spread(step, carry, source=source, target=target, n=n, half=half, first=first):
                other = half * half_size + lax.rem(place + first + zigzag(step), half_size)
                along = lax.rem(other, 2) == 0
                there = jnp.where(along, col_x, row_y) if n == 1 else jnp.where(along, row_y, col_x)

                @pl.when(other != place)
                def _():
                    pltpu.make_async_remote_copy(
                        src_ref=source.at[0, :, channels(other)],
                        dst_ref=target.at[there, z_hi, span],
                        send_sem=send_sem.at[n], recv_sem=recv_sem.at[n, my_half],
                        device_id=at_place(other), device_id_type=MESH,
                    ).start()

                return carry
            lax.fori_loop(0, half_size, spread, 0)

    def gather(n, half):
        target = arrays[n][1]
        here, peer = (query_at, query_peer) if n == 1 else (key_at, key_peer)
        sems = (key_sems, query_sems, value_sems)[n]
        block = target.at[here, pl.ds(half * near, near)]
        pltpu.make_async_copy(block, block, recv_sem.at[n, half]).wait()
        copies = []
        for turn in range(1, side):
            copy = pltpu.make_async_remote_copy(
                src_ref=block, dst_ref=block, send_sem=sems.at[0, half, turn],
                recv_sem=sems.at[1, half, turn], device_id=peer(turn), device_id_type=MESH,
            )
            copy.start()
            copies.append(copy)
        return copies

    first = [gather(n, 1) for n in range(3)]
    for copy in small:
        copy.wait()

    block = side * near * tok
    lanes = lax.broadcasted_iota(jnp.int32, (1, 2 * block), 1)
    inside = lax.rem(lanes, block)
    start = plane + (lax.div(inside, near * tok) - key_at) * key_step
    bias = []
    for half in range(2):
        position = start * rows + half * near * tok + lax.rem(inside, near * tok)
        bias.append([
            jnp.where(
                position < jnp.where(lanes < block, counts_s[2 * j], counts_s[2 * j + 1]),
                0.0, MASKED,
            )
            for j in range(pairs)
        ])
    row_ids = lax.broadcasted_iota(jnp.int32, (many, many), 0)
    lane_ids = lax.broadcasted_iota(jnp.int32, (many, many), 1)
    diagonal = row_ids == lane_ids
    row_ids = lax.broadcasted_iota(jnp.int32, (many, 2 * block), 0)
    lane_ids = lax.broadcasted_iota(jnp.int32, (many, 2 * block), 1)
    later = jnp.where((lax.rem(lax.div(row_ids, tok), 2) == 0) & (lane_ids >= block), MASKED, 0.0)
    factor = math.log2(math.e) / math.sqrt(HEAD_DIM)

    def flat(tiles):
        wide = tiles.astype(jnp.float32)
        return wide.reshape(math.prod(wide.shape[:-1]), HEAD_DIM).astype(jnp.bfloat16)

    def flatten(source, target, half):
        for c in range(spans):
            target[half, c * block : (c + 1) * block] = flat(
                source[:, half * near : (half + 1) * near, c]
            )

    def landed(copies):
        for copy in copies:
            copy.wait_recv()

    second = [gather(0, 0), gather(1, 0)]
    landed(first[0])
    flatten(key_all, keys_flat, 1)
    landed(first[2])
    flatten(value_all, values_flat, 1)
    second.append(gather(2, 0))
    landed(first[1])
    landed(second[0])
    flatten(key_all, keys_flat, 0)
    landed(second[1])

    def exchange(source, target, sems, at):
        copies = []
        for turn in range(1, side):
            copy = pltpu.make_async_remote_copy(
                src_ref=source(lax.rem(query_at + turn, side)), dst_ref=target(turn - 1),
                send_sem=sems.at[0, at, turn], recv_sem=sems.at[1, at, turn],
                device_id=query_peer(turn), device_id_type=MESH,
            )
            copy.start()
            copies.append(copy)
        return copies

    def score(half):
        totals = []
        for j in range(pairs):
            wide = 2 * (j + 1) * block
            queries = flat(query_all[:, half * near : (half + 1) * near, 2 * j : 2 * j + 2])
            scores = []
            for part_of in range(2):
                raw = lax.dot_general(
                    queries, keys_flat[part_of, :wide], (((1,), (1,)), ((), ())),
                    preferred_element_type=jnp.float32,
                ) * factor
                for i in range(j + 1):
                    piece = raw[:, 2 * i * block : 2 * (i + 1) * block] + bias[part_of][i]
                    scores.append(piece + later if i == j else piece)
            top = functools.reduce(jnp.maximum, scores)
            top = jnp.maximum(jnp.max(top, axis=1, keepdims=True), LOWEST)
            weights = [jnp.exp2(piece - top) for piece in scores]
            total = jnp.sum(functools.reduce(jnp.add, weights), axis=1, keepdims=True)
            total = jnp.maximum(total, TINY)
            for at, piece in enumerate(weights):
                i = at % (j + 1)
                chances[half, j, at // (j + 1), :, 2 * i * block : 2 * (i + 1) * block] = (
                    piece.astype(jnp.bfloat16)
                )
            both = jnp.sum(jnp.where(diagonal, top + jnp.log2(total), 0.0), axis=0, keepdims=True)
            lse[half, j : j + 1, :] = both
            lse[half, pairs + j : pairs + j + 1, :] = both
            totals.append(1.0 / total)
        return totals, exchange(
            lambda other: lse.at[half], lambda n: lse_in.at[half, n], lse_sems, half
        )

    def weigh(half, j, part_of):
        wide = 2 * (j + 1) * block
        return jnp.dot(
            chances[half, j, part_of, :, :wide], values_flat[part_of, :wide],
            preferred_element_type=jnp.float32,
        )

    scored = [score(0), score(1)]
    for half in range(2):
        for j in range(pairs):
            summed[half, j] = weigh(half, j, 1)
    landed(second[2])
    flatten(value_all, values_flat, 0)

    def mix(half):
        for j in range(pairs):
            mixture = (summed[half, j] + weigh(half, j, 0)) * scored[half][0][j]
            part[half, :, :, 2 * j : 2 * j + 2] = mixture.reshape(
                side, near, 2, tok, HEAD_DIM
            ).astype(jnp.bfloat16)
        return [
            exchange(
                lambda other: part.at[half, other, z], lambda n: part_in.at[half, n, z],
                part_sems, half * near + z,
            )
            for z in range(near)
        ]

    cut = 2 * tok
    row_ids = lax.broadcasted_iota(jnp.int32, (cut, many), 0)
    lane_ids = lax.broadcasted_iota(jnp.int32, (cut, many), 1) - query_at * near * cut

    def share_out(half):
        landed(scored[half][1])
        tables = [lse[half]] + [lse_in[half, n] for n in range(side - 1)]
        top = functools.reduce(jnp.maximum, tables)
        tables = [jnp.exp2(table - top) for table in tables]
        total = functools.reduce(jnp.add, tables)
        tables = [table / total for table in tables]
        return [
            [
                jnp.concatenate([
                    jnp.sum(
                        jnp.where(lane_ids == row_ids + z * cut, table[j : j + 1], 0.0),
                        axis=1, keepdims=True,
                    )
                    for j in range(pairs)
                ], axis=0)
                for table in tables
            ]
            for z in range(near)
        ]

    parts = mix(0)
    shares = share_out(0)
    gates = jnp.concatenate([
        jnp.broadcast_to(gate_v[pl.ds(levels_s[i], 1), :], (tok, HEAD_DIM)) for i in range(spans)
    ], axis=0)
    parts += mix(1)
    shares += share_out(1)

    for level in range(z_far):
        half, z = level // near, level % near
        landed(parts[level])
        attended = jnp.zeros((spans * tok, HEAD_DIM), jnp.float32)
        for n in range(side):
            tile = part[half, query_at, z] if n == 0 else part_in[half, n - 1, z]
            tile = tile.astype(jnp.float32).reshape(spans * tok, HEAD_DIM)
            attended = attended + shares[level][n] * tile
        mean = jnp.mean(attended * attended, axis=1, keepdims=True)
        normed = attended * lax.rsqrt(mean + EPSILON) * gates
        mixed[level] = normed.reshape(spans, tok, HEAD_DIM).astype(jnp.bfloat16)

        def send_back(step, carry, level=level):
            other_span = lax.rem(span + step, spans)
            other = level * spans + other_span

            @pl.when(other != place)
            def _():
                pltpu.make_async_remote_copy(
                    src_ref=mixed.at[level, other_span],
                    dst_ref=out_ref.at[0, :, channels(place)],
                    send_sem=out_send, recv_sem=out_recv,
                    device_id=at_place(other), device_id_type=MESH,
                ).start()

            @pl.when(other == place)
            def _():
                pltpu.make_async_copy(
                    mixed.at[level, other_span], out_ref.at[0, :, channels(place)], out_recv
                ).start()

            return carry

        lax.fori_loop(0, spans, send_back, 0)

    sent = [copy for group in first + second + parts for copy in group]
    sent += scored[0][1] + scored[1][1]
    for source, target, n in arrays:
        rest = source.at[0, :, pl.ds(0, (column - 1) * HEAD_DIM)]
        pltpu.make_async_copy(rest, rest, send_sem.at[n]).wait()
    for copy in sent:
        copy.wait_send()
    rest = out_ref.at[0, :, pl.ds(0, (column - 1) * HEAD_DIM)]
    pltpu.make_async_copy(rest, rest, out_send).wait()
    pltpu.make_async_copy(out_ref, out_ref, out_recv).wait()


def body(query_rows, key_rows, value_rows, counts, levels, gate_table):
    spans = lax.axis_size("span")
    seq_size = lax.axis_size("seq")
    tok, width = query_rows.shape[1:]
    column = width // HEAD_DIM
    z_far = column // spans
    side = math.isqrt(seq_size // z_far)
    many = side * z_far * tok
    pairs = spans // 2
    bf16, f32 = jnp.bfloat16, jnp.float32
    gathered = pltpu.VMEM((side, z_far, spans, tok, HEAD_DIM), bf16)
    flat = pltpu.VMEM((2, spans * many // 2, HEAD_DIM), bf16)
    dma = pltpu.SemaphoreType.DMA
    hbm = pl.BlockSpec(memory_space=pltpu.HBM)
    return pl.pallas_call(
        functools.partial(kernel, spans, z_far, side, tok),
        out_shape=jax.ShapeDtypeStruct(query_rows.shape, bf16),
        in_specs=[hbm] * 6,
        out_specs=pl.BlockSpec(memory_space=pl.ANY),
        scratch_shapes=[
            gathered, gathered, gathered, flat, flat,
            pltpu.VMEM((2, pairs, 2, many, spans * many // 2), bf16),
            pltpu.VMEM((2, pairs, many, HEAD_DIM), f32),
            pltpu.VMEM((2, side, z_far // 2, spans, tok, HEAD_DIM), bf16),
            pltpu.VMEM((2, side - 1, z_far // 2, spans, tok, HEAD_DIM), bf16),
            pltpu.VMEM((2, 2 * pairs, many), f32),
            pltpu.VMEM((2, side - 1, 2 * pairs, many), f32),
            pltpu.VMEM((z_far, spans, tok, HEAD_DIM), bf16),
            pltpu.VMEM((gate_table.shape[0], HEAD_DIM), f32),
            pltpu.SMEM(counts.shape, jnp.int32),
            pltpu.SMEM(levels.shape, jnp.int32),
            dma((3,)), dma((3, 2)),
            dma((2, 2, side)), dma((2, 2, side)), dma((2, 2, side)),
            dma((2, z_far, side)), dma((2, 2, side)),
            dma, dma, dma((3,)),
        ],
        compiler_params=pltpu.CompilerParams(
            collective_id=0, has_side_effects=True, vmem_limit_bytes=VMEM_BYTES
        ),
        cost_estimate=pl.CostEstimate(
            flops=600_000_000, bytes_accessed=1_000_000, transcendentals=700_000
        ),
    )(*[
        pltpu.with_memory_space_constraint(array, pltpu.HBM)
        for array in (query_rows, key_rows, value_rows, counts, levels, gate_table)
    ])


def solution(mesh):
    placed = (P("span", "seq", None), P("span", "seq", None), P("span", "seq", None), P(), P(), P())
    return jax.shard_map(
        body, mesh=mesh, in_specs=placed, out_specs=P("span", "seq", None), check_vma=False
    )
```

time: 49 us -> 51.3 us (1.047)
  Pallas kernels: 48.3 us -> 50.6 us
    pallas_call x1, Pallas kernels: 48.3 us -> 50.6 us  [body(): pl.pallas_call(functools.partial(kernel, spans, z_far, side, tok), out_sh...]
where the time goes in v3:
time: 51.3 us; the launch traced here: 51.2 us
  Pallas kernels  50.6 us (99%)
  local copies, waits for them, and re-layouts  0.63 us (1%)
    pallas_call x1, Pallas kernels, body(): pl.pallas_call(functools.partial(kernel, spans, z_far, side, tok), out_sh...  50.6 us

profile of v3, /device:TPU:1, one launch (start us, length us, event | category | flops | bytes accessed | tf_op | source)
XLA Modules:
  0.0 51.2 jit_solution(5286376196924023183)
XLA Ops:
  0.0 50.6 %shard_map.64 = bf16[1,8,4096]{2,1,0:T(8,128)(2,1)S(1)} custom-call(bf16[1,8,4096]{2,1,0:T(8,128)(2,1)} %query_ref.1, bf16[1,8,4096]{2,1,0:T(8,128)(2,1)} %key_ref.1, bf16[1,8,4096]{2,1,0:T(8,128)(2,1)} %value_ref.1, s32[8]{0:T(128)} %counts_ref.1, s32[8]{0:T(128)} %levels_ref.1, f32[64,4096]{1,0:T(8,128)} %gate_ref.1), custom_call_target="tpu_custom_call" | custom-call | flops 600000000 | bytes 1000000 | tf_op jit(solution)/shard_map/pallas_call | solution.py:349
  50.6 0.6 %copy.8 = bf16[1,8,4096]{2,1,0:T(8,128)(2,1)} copy(bf16[1,8,4096]{2,1,0:T(8,128)(2,1)S(1)} %shard_map.64) | data formatting | bytes 131072

commit v4 on v3

--- a/solution.py
+++ b/solution.py
@@ -93,25 +93,18 @@
         half = lax.div(step + 1, 2)
         return jnp.where(lax.rem(step, 2) == 0, half, -half)
 
-    for half in (1, 0):
-        first = jnp.where(my_half == half, half_size // 2, 0) + half_size
-        for source, target, n in arrays:
-            def spread(step, carry, source=source, target=target, n=n, half=half, first=first):
-                other = half * half_size + lax.rem(place + first + zigzag(step), half_size)
-                along = lax.rem(other, 2) == 0
-                there = jnp.where(along, col_x, row_y) if n == 1 else jnp.where(along, row_y, col_x)
-
-                @pl.when(other != place)
-                def _():
-                    pltpu.make_async_remote_copy(
-                        src_ref=source.at[0, :, channels(other)],
-                        dst_ref=target.at[there, z_hi, span],
-                        send_sem=send_sem.at[n], recv_sem=recv_sem.at[n, my_half],
-                        device_id=at_place(other), device_id_type=MESH,
-                    ).start()
-
-                return carry
-            lax.fori_loop(0, half_size, spread, 0)
+    for source, target, n in arrays:
+        def spread(step, carry, source=source, target=target, n=n):
+            other = other_place(step)
+            along = lax.rem(other, 2) == 0
+            there = jnp.where(along, col_x, row_y) if n == 1 else jnp.where(along, row_y, col_x)
+            pltpu.make_async_remote_copy(
+                src_ref=source.at[0, :, channels(other)], dst_ref=target.at[there, z_hi, span],
+                send_sem=send_sem.at[n], recv_sem=recv_sem.at[n, my_half],
+                device_id=at_place(other), device_id_type=MESH,
+            ).start()
+            return carry
+        lax.fori_loop(0, column - 1, spread, 0)
 
     def gather(n, half):
         target = arrays[n][1]
@@ -129,7 +122,10 @@
             copies.append(copy)
         return copies
 
-    first = [gather(n, 1) for n in range(3)]
+    first = [gather(0, 1), gather(1, 1)]
+    second = [gather(0, 0), gather(1, 0)]
+    first.append(gather(2, 1))
+    second.append(gather(2, 0))
     for copy in small:
         copy.wait()
 
@@ -169,12 +165,10 @@
         for copy in copies:
             copy.wait_recv()
 
-    second = [gather(0, 0), gather(1, 0)]
     landed(first[0])
     flatten(key_all, keys_flat, 1)
     landed(first[2])
     flatten(value_all, values_flat, 1)
-    second.append(gather(2, 0))
     landed(first[1])
     landed(second[0])
     flatten(key_all, keys_flat, 0)
@@ -298,7 +292,7 @@
         mixed[level] = normed.reshape(spans, tok, HEAD_DIM).astype(jnp.bfloat16)
 
         def send_back(step, carry, level=level):
-            other_span = lax.rem(span + step, spans)
+            other_span = step
             other = level * spans + other_span
 
             @pl.when(other != place)

time: 51.3 us -> 48.1 us (0.938)
  Pallas kernels: 50.6 us -> 47.4 us
    pallas_call x1, Pallas kernels: 50.6 us -> 47.4 us  [body(): pl.pallas_call(functools.partial(kernel, spans, z_far, side, tok), out_sh...]
where the time goes in v4:
time: 48.1 us; the launch traced here: 48 us
  Pallas kernels  47.4 us (99%)
  local copies, waits for them, and re-layouts  0.63 us (1%)
    pallas_call x1, Pallas kernels, body(): pl.pallas_call(functools.partial(kernel, spans, z_far, side, tok), out_sh...  47.4 us

profile of v4, /device:TPU:1, one launch (start us, length us, event | category | flops | bytes accessed | tf_op | source)
XLA Modules:
  0.0 48.0 jit_solution(11964202021639067248)
XLA Ops:
  0.0 47.4 %shard_map.64 = bf16[1,8,4096]{2,1,0:T(8,128)(2,1)S(1)} custom-call(bf16[1,8,4096]{2,1,0:T(8,128)(2,1)} %query_ref.1, bf16[1,8,4096]{2,1,0:T(8,128)(2,1)} %key_ref.1, bf16[1,8,4096]{2,1,0:T(8,128)(2,1)} %value_ref.1, s32[8]{0:T(128)} %counts_ref.1, s32[8]{0:T(128)} %levels_ref.1, f32[64,4096]{1,0:T(8,128)} %gate_ref.1), custom_call_target="tpu_custom_call" | custom-call | flops 600000000 | bytes 1000000 | tf_op jit(solution)/shard_map/pallas_call | solution.py:343
  47.4 0.6 %copy.8 = bf16[1,8,4096]{2,1,0:T(8,128)(2,1)} copy(bf16[1,8,4096]{2,1,0:T(8,128)(2,1)S(1)} %shard_map.64) | data formatting | bytes 131072

commit v5 on v4

--- a/solution.py
+++ b/solution.py
@@ -20,9 +20,9 @@
 def kernel(
     spans, z_far, side, tok,
     query_ref, key_ref, value_ref, counts_ref, levels_ref, gate_ref, out_ref,
-    key_all, query_all, value_all, keys_flat, values_flat, chances, summed, part, part_in, lse, lse_in,
+    key_rows, query_rows, paired, paired_in, key_all, query_all, value_all, keys_flat, values_flat, chances, summed, part, part_in, lse, lse_in,
     mixed, gate_v, counts_s, levels_s,
-    send_sem, recv_sem, key_sems, query_sems, value_sems, part_sems, lse_sems,
+    load_sems, send_sem, recv_sem, key_sems, query_sems, value_sems, part_sems, lse_sems,
     out_send, out_recv, small_sems,
 ):
     column = spans * z_far
@@ -74,12 +74,14 @@
         pl.semaphore_signal(barrier, inc=1, device_id=key_peer(turn), device_id_type=MESH)
         pl.semaphore_signal(barrier, inc=1, device_id=query_peer(turn), device_id_type=MESH)
 
-    arrays = ((key_ref, key_all, 0), (query_ref, query_all, 1), (value_ref, value_all, 2))
-    for source, target, n in arrays:
-        here = query_at if n == 1 else key_at
-        pltpu.make_async_copy(
-            source.at[0, :, channels(place)], target.at[here, z_hi, span], recv_sem.at[n, my_half]
-        ).start()
+    loads = []
+    for n, (source, target) in enumerate(((key_ref, key_rows), (query_ref, query_rows))):
+        copy = pltpu.make_async_copy(source, target, load_sems.at[n])
+        copy.start()
+        loads.append(copy)
+    pltpu.make_async_copy(
+        value_ref.at[0, :, channels(place)], value_all.at[key_at, z_hi, span], recv_sem.at[1, my_half]
+    ).start()
     small = [
         pltpu.make_async_copy(counts_ref, counts_s, small_sems.at[0]),
         pltpu.make_async_copy(levels_ref, levels_s, small_sems.at[1]),
@@ -87,45 +89,69 @@
     ]
     for copy in small:
         copy.start()
+    for n, source in enumerate((key_rows, query_rows)):
+        loads[n].wait()
+        for head in range(column):
+            paired[head, n] = source[0, :, head * HEAD_DIM : (head + 1) * HEAD_DIM]
+    pltpu.make_async_copy(
+        paired.at[place], paired_in.at[z_hi, span], recv_sem.at[0, my_half]
+    ).start()
     pl.semaphore_wait(barrier, column - 1 + 2 * (side - 1))
 
-    def zigzag(step):
-        half = lax.div(step + 1, 2)
-        return jnp.where(lax.rem(step, 2) == 0, half, -half)
-
-    for source, target, n in arrays:
-        def spread(step, carry, source=source, target=target, n=n):
-            other = other_place(step)
-            along = lax.rem(other, 2) == 0
-            there = jnp.where(along, col_x, row_y) if n == 1 else jnp.where(along, row_y, col_x)
-            pltpu.make_async_remote_copy(
-                src_ref=source.at[0, :, channels(other)], dst_ref=target.at[there, z_hi, span],
-                send_sem=send_sem.at[n], recv_sem=recv_sem.at[n, my_half],
-                device_id=at_place(other), device_id_type=MESH,
-            ).start()
-            return carry
-        lax.fori_loop(0, column - 1, spread, 0)
+    def spread_pairs(step, carry):
+        other = other_place(step)
+        pltpu.make_async_remote_copy(
+            src_ref=paired.at[other], dst_ref=paired_in.at[z_hi, span],
+            send_sem=send_sem.at[0], recv_sem=recv_sem.at[0, my_half],
+            device_id=at_place(other), device_id_type=MESH,
+        ).start()
+        return carry
+
+    def spread_values(step, carry):
+        other = other_place(step)
+        there = jnp.where(lax.rem(other, 2) == 0, row_y, col_x)
+        pltpu.make_async_remote_copy(
+            src_ref=value_ref.at[0, :, channels(other)], dst_ref=value_all.at[there, z_hi, span],
+            send_sem=send_sem.at[1], recv_sem=recv_sem.at[1, my_half],
+            device_id=at_place(other), device_id_type=MESH,
+        ).start()
+        return carry
+
+    lax.fori_loop(0, column - 1, spread_pairs, 0)
+    lax.fori_loop(0, column - 1, spread_values, 0)
 
     def gather(n, half):
-        target = arrays[n][1]
+        target, sems = ((key_all, key_sems), (query_all, query_sems), (value_all, value_sems))[n]
         here, peer = (query_at, query_peer) if n == 1 else (key_at, key_peer)
-        sems = (key_sems, query_sems, value_sems)[n]
-        block = target.at[here, pl.ds(half * near, near)]
-        pltpu.make_async_copy(block, block, recv_sem.at[n, half]).wait()
+        slab = pl.ds(half * near, near)
+        block = target.at[here, slab]
+        source = block if n == 2 else paired_in.at[slab, :, n]
         copies = []
         for turn in range(1, side):
             copy = pltpu.make_async_remote_copy(
-                src_ref=block, dst_ref=block, send_sem=sems.at[0, half, turn],
+                src_ref=source, dst_ref=block, send_sem=sems.at[0, half, turn],
                 recv_sem=sems.at[1, half, turn], device_id=peer(turn), device_id_type=MESH,
             )
             copy.start()
             copies.append(copy)
+        if n < 2:
+            target[here, half * near : (half + 1) * near] = paired_in[
+                half * near : (half + 1) * near, :, n
+            ]
         return copies
 
-    first = [gather(0, 1), gather(1, 1)]
-    second = [gather(0, 0), gather(1, 0)]
-    first.append(gather(2, 1))
-    second.append(gather(2, 0))
+    def arrive(target, n, half):
+        block = target.at[pl.ds(half * near, near)]
+        pltpu.make_async_copy(block, block, recv_sem.at[n, half]).wait()
+
+    first, second = [], []
+    for half, copies in ((1, first), (0, second)):
+        arrive(paired_in, 0, half)
+        copies.append(gather(0, half))
+        copies.append(gather(1, half))
+    for half, copies in ((1, first), (0, second)):
+        arrive(value_all.at[key_at], 1, half)
+        copies.append(gather(2, half))
     for copy in small:
         copy.wait()
 
@@ -212,7 +238,6 @@
                 )
             both = jnp.sum(jnp.where(diagonal, top + jnp.log2(total), 0.0), axis=0, keepdims=True)
             lse[half, j : j + 1, :] = both
-            lse[half, pairs + j : pairs + j + 1, :] = both
             totals.append(1.0 / total)
         return totals, exchange(
             lambda other: lse.at[half], lambda n: lse_in.at[half, n], lse_sems, half
@@ -316,9 +341,10 @@
 
     sent = [copy for group in first + second + parts for copy in group]
     sent += scored[0][1] + scored[1][1]
-    for source, target, n in arrays:
-        rest = source.at[0, :, pl.ds(0, (column - 1) * HEAD_DIM)]
-        pltpu.make_async_copy(rest, rest, send_sem.at[n]).wait()
+    rest = paired.at[pl.ds(0, column - 1)]
+    pltpu.make_async_copy(rest, rest, send_sem.at[0]).wait()
+    rest = value_ref.at[0, :, pl.ds(0, (column - 1) * HEAD_DIM)]
+    pltpu.make_async_copy(rest, rest, send_sem.at[1]).wait()
     for copy in sent:
         copy.wait_send()
     rest = out_ref.at[0, :, pl.ds(0, (column - 1) * HEAD_DIM)]
@@ -346,18 +372,22 @@
         in_specs=[hbm] * 6,
         out_specs=pl.BlockSpec(memory_space=pl.ANY),
         scratch_shapes=[
+            pltpu.VMEM(key_rows.shape, bf16),
+            pltpu.VMEM(query_rows.shape, bf16),
+            pltpu.VMEM((column, 2, tok, HEAD_DIM), bf16),
+            pltpu.VMEM((z_far, spans, 2, tok, HEAD_DIM), bf16),
             gathered, gathered, gathered, flat, flat,
             pltpu.VMEM((2, pairs, 2, many, spans * many // 2), bf16),
             pltpu.VMEM((2, pairs, many, HEAD_DIM), f32),
             pltpu.VMEM((2, side, z_far // 2, spans, tok, HEAD_DIM), bf16),
             pltpu.VMEM((2, side - 1, z_far // 2, spans, tok, HEAD_DIM), bf16),
-            pltpu.VMEM((2, 2 * pairs, many), f32),
-            pltpu.VMEM((2, side - 1, 2 * pairs, many), f32),
+            pltpu.VMEM((2, pairs, many), f32),
+            pltpu.VMEM((2, side - 1, pairs, many), f32),
             pltpu.VMEM((z_far, spans, tok, HEAD_DIM), bf16),
             pltpu.VMEM((gate_table.shape[0], HEAD_DIM), f32),
             pltpu.SMEM(counts.shape, jnp.int32),
             pltpu.SMEM(levels.shape, jnp.int32),
-            dma((3,)), dma((3, 2)),
+            dma((2,)), dma((2,)), dma((2, 2)),
             dma((2, 2, side)), dma((2, 2, side)), dma((2, 2, side)),
             dma((2, z_far, side)), dma((2, 2, side)),
             dma, dma, dma((3,)),

time: 48.1 us -> 47.9 us (level)
  no operation moved by 1% of the time
where the time goes in v5:
time: 47.9 us; the launch traced here: 47.8 us
  Pallas kernels  47.1 us (98%)
  local copies, waits for them, and re-layouts  0.63 us (1%)
    pallas_call x1, Pallas kernels, body(): pl.pallas_call(functools.partial(kernel, spans, z_far, side, tok), out_sh...  47.1 us

profile of v5, /device:TPU:1, one launch (start us, length us, event | category | flops | bytes accessed | tf_op | source)
XLA Modules:
  0.0 47.8 jit_solution(3131804437093515524)
XLA Ops:
  0.0 47.1 %shard_map.64 = bf16[1,8,4096]{2,1,0:T(8,128)(2,1)S(1)} custom-call(bf16[1,8,4096]{2,1,0:T(8,128)(2,1)} %query_ref.1, bf16[1,8,4096]{2,1,0:T(8,128)(2,1)} %key_ref.1, bf16[1,8,4096]{2,1,0:T(8,128)(2,1)} %value_ref.1, s32[8]{0:T(128)} %counts_ref.1, s32[8]{0:T(128)} %levels_ref.1, f32[64,4096]{1,0:T(8,128)} %gate_ref.1), custom_call_target="tpu_custom_call" | custom-call | flops 600000000 | bytes 1000000 | tf_op jit(solution)/shard_map/pallas_call | solution.py:369
  47.2 0.6 %copy.8 = bf16[1,8,4096]{2,1,0:T(8,128)(2,1)} copy(bf16[1,8,4096]{2,1,0:T(8,128)(2,1)S(1)} %shard_map.64) | data formatting | bytes 131072

commit v6 on v5

--- a/solution.py
+++ b/solution.py
@@ -317,7 +317,7 @@
         mixed[level] = normed.reshape(spans, tok, HEAD_DIM).astype(jnp.bfloat16)
 
         def send_back(step, carry, level=level):
-            other_span = step
+            other_span = step + 1 - 2 * lax.rem(step, 2)
             other = level * spans + other_span
 
             @pl.when(other != place)

time: 47.9 us -> 47.8 us (level)
  no operation moved by 1% of the time
where the time goes in v6:
time: 47.8 us; the launch traced here: 47.6 us
  Pallas kernels  47 us (98%)
  local copies, waits for them, and re-layouts  0.63 us (1%)
    pallas_call x1, Pallas kernels, body(): pl.pallas_call(functools.partial(kernel, spans, z_far, side, tok), out_sh...  47 us

profile of v6, /device:TPU:1, one launch (start us, length us, event | category | flops | bytes accessed | tf_op | source)
XLA Modules:
  0.0 47.6 jit_solution(4010926959739933108)
XLA Ops:
  0.0 47.0 %shard_map.64 = bf16[1,8,4096]{2,1,0:T(8,128)(2,1)S(1)} custom-call(bf16[1,8,4096]{2,1,0:T(8,128)(2,1)} %query_ref.1, bf16[1,8,4096]{2,1,0:T(8,128)(2,1)} %key_ref.1, bf16[1,8,4096]{2,1,0:T(8,128)(2,1)} %value_ref.1, s32[8]{0:T(128)} %counts_ref.1, s32[8]{0:T(128)} %levels_ref.1, f32[64,4096]{1,0:T(8,128)} %gate_ref.1), custom_call_target="tpu_custom_call" | custom-call | flops 600000000 | bytes 1000000 | tf_op jit(solution)/shard_map/pallas_call | solution.py:369
  47.0 0.6 %copy.8 = bf16[1,8,4096]{2,1,0:T(8,128)(2,1)} copy(bf16[1,8,4096]{2,1,0:T(8,128)(2,1)S(1)} %shard_map.64) | data formatting | bytes 131072
